TPU v7x, 32 devices: a whole 2x2x4 slice. The times are simulated.
32 devices in a mesh: tile: 16 (over z, y, core), pair: 2 (over x).
Axes of the slice: x: 2, y: 2, z: 4, core: 2. Of those that a mesh axis runs over, the one named last changes fastest.
Arguments:
- state: bfloat16 [2, 32, 256, 512], P('pair', None, 'tile'), may hold values from -6 to 6
- target: bfloat16 [2, 32, 256, 512], P('pair', None, 'tile'), may hold values from -6 to 6
- perturbation: bfloat16 [2, 32, 256, 512], P('pair', None, 'tile'), may hold values from -4 to 4
- legendre: bfloat16 [256, 256, 256], P('tile'), may hold values from -0.375 to 0.375
- damp: float32 [32, 256], replicated, may hold values from 0.3 to 3
Outputs:
- grad_state: float32 [2, 32, 256, 512], P('pair', None, 'tile')
- grad_damp: float32 [32, 256], replicated
All inputs are finite; a program needn't handle non-finite values.
Results may differ from a plain program's by a relative error of at most 0.007.
Values may be sent and summed in bfloat16 or wider, within the bound.
A program may use at most 64 MiB of HBM per device.

v0:
```python
import math

import jax
import jax.numpy as jnp
from jax import lax
from jax.sharding import PartitionSpec as P

NLON = 512
M = 256


def swapped(value, axis, distance):
    mask = 2**distance
    pairs = [(source, source ^ mask) for source in range(lax.axis_size(axis))]
    return lax.ppermute(value, axis, pairs)


def fourier_table(length, waves):
    points = jnp.arange(length, dtype=jnp.int32)
    orders = jnp.arange(waves, dtype=jnp.int32)
    phase = points[:, None] * orders[None, :] % length
    angle = phase.astype(jnp.float32) * (2.0 * math.pi / length)
    stacked = jnp.stack([jnp.cos(angle), -jnp.sin(angle)], axis=1)
    return (stacked * length ** (-0.5)).astype(jnp.bfloat16)


def body(state, target, perturbation, legendre, damp):
    table = fourier_table(NLON, M)
    waves_dev = legendre.shape[0]
    first = lax.axis_index("tile") * waves_dev
    wave_ids = first + jnp.arange(waves_dev, dtype=jnp.int32)
    degree = jnp.arange(legendre.shape[1], dtype=jnp.int32)
    masked = jnp.where(
        degree[None, :, None] >= wave_ids[:, None, None], legendre, jnp.zeros_like(legendre)
    )
    gain = damp[None, :, None, None, :]

    def analyse(grid):
        return jnp.einsum(
            "blgj,jrm->blrmg", grid, table, preferred_element_type=jnp.float32
        ).astype(jnp.bfloat16)

    def synthesise(spec):
        return jnp.einsum("blrmg,jrm->blgj", spec, table, preferred_element_type=jnp.float32)

    def spectral_pass(piece, sender):
        coef = jnp.einsum("blrmg,mng->blrmn", piece, masked, preferred_element_type=jnp.float32)
        filtered = (coef * gain).astype(jnp.bfloat16)
        back = jnp.einsum(
            "blrmn,mng->blrmg", filtered, masked, preferred_element_type=jnp.float32
        ).astype(jnp.bfloat16)
        return (sender(back), coef)

    def to_grid(back):
        return lax.all_to_all(back, "tile", split_axis=4, concat_axis=3, tiled=True)

    def spectral(grid_coef):
        spec = lax.all_to_all(grid_coef, "tile", split_axis=3, concat_axis=4, tiled=True)
        return spectral_pass(spec, to_grid)

    back_grid, coef = spectral(analyse(state))
    bent = jnp.tanh(synthesise(back_grid))
    advanced = (state.astype(jnp.float32) + bent + perturbation.astype(jnp.float32)).astype(
        jnp.bfloat16
    )
    partner = swapped(advanced, "pair", 0)
    mine = advanced.astype(jnp.float32)
    miss = mine - target.astype(jnp.float32)
    spread = mine - partner.astype(jnp.float32)
    grad_adv = 0.5 * miss * lax.rsqrt(miss * miss + 1.0) - 0.25 * spread * lax.rsqrt(
        spread * spread + 1.0
    )
    grad_wave = (grad_adv * (1.0 - bent * bent)).astype(jnp.bfloat16)
    grad_fourier, grad_coef = spectral(analyse(grad_wave))
    grad_state = grad_adv + synthesise(grad_fourier)
    partial_sum = jnp.sum(coef * grad_coef, axis=(0, 2, 3))
    total = lax.psum(partial_sum, ("tile", "pair"))
    members = state.shape[0] * lax.axis_size("pair")
    return (grad_state, total * (members * M) ** (-0.5))


def solution(mesh):
    placed = (
        P("pair", None, "tile", None),
        P("pair", None, "tile", None),
        P("pair", None, "tile", None),
        P("tile", None, None),
        P(),
    )
    return jax.shard_map(
        body,
        mesh=mesh,
        in_specs=placed,
        out_specs=(P("pair", None, "tile", None), P()),
        check_vma=False,
    )
```

profile of v0, /device:TPU:0, one launch (start us, length us, event | category | flops | bytes accessed | tf_op | source)
XLA Modules:
  0.0 177.8 jit_solution(7167548998546380045)
XLA Ops:
  0.6 2.1 %sine_negate_fusion = (f32[512,1,256]{2,0,1:T(8,128)S(1)}, f32[512,1,256]{2,0,1:T(8,128)S(1)}) fusion(), kind=kLoop, calls=%fused_computation.61 | loop fusion | flops 1966080 | bytes 1048576 | tf_op jit(solution)/shard_map/neg | solution.py:23
  2.7 0.1 fusion.36
  2.8 0.5 fusion.34
  3.3 3.0 %copy.28 = bf16[1,32,2,256,16]{1,4,2,0,3:T(8,128)(2,1)S(1)} copy(bf16[1,32,2,256,16]{3,1,4,2,0:T(8,128)(2,1)S(1)} %fusion.34) | data formatting | bytes 1048576 | tf_op jit(solution)/shard_map/convert_element_type | solution.py:41
  6.3 2.7 %reshape.161 = bf16[16,2,8192]{2,1,0:T(2,128)(2,1)} reshape(bf16[256,1,2,16,32]{4,3,2,1,0:T(8,128)(2,1)S(1)} %bitcast.126) | data formatting | bytes 1048576
  9.0 7.4 %all-to-all-start = ((bf16[16,2,8192]{2,1,0:T(2,128)(2,1)}), bf16[16,2,8192]{2,1,0:T(2,128)(2,1)S(1)}, u32[]{:S(2)}, u32[]{:S(2)}) async-start(bf16[16,2,8192]{2,1,0:T(2,128)(2,1)} %reshape.161), calls=%async_computation | async-start | bytes 1048576 | tf_op jit(solution)/shard_map/all_to_all | solution.py:58
  16.4 0.1 iota_compare_fusion
  16.4 14.4 %all-to-all-done = bf16[16,2,8192]{2,1,0:T(2,128)(2,1)S(1)} async-done(((bf16[16,2,8192]{2,1,0:T(2,128)(2,1)}), bf16[16,2,8192]{2,1,0:T(2,128)(2,1)S(1)}, u32[]{:S(2)}, u32[]{:S(2)}) %all-to-all-start) | async-done | bytes 524320 | tf_op jit(solution)/shard_map/all_to_all | solution.py:58
  30.8 1.0 reshape.162
  31.9 0.4 copy.29
  32.2 0.6 copy.30
  32.8 1.0 copy-done.5
  33.8 2.5 %fusion.10 = f32[1,32,2,16,256]{4,1,2,3,0:T(8,128)S(1)} fusion(bf16[32,2,16,256]{0,3,2,1:T(8,128)(2,1)S(1)} %bitcast.141, bf16[16,256,256]{2,1,0:T(8,128)(2,1)S(1)} %copy-done.5, pred[16,256]{1,0:T(8,128)(4,1)S(1)} %iota_compare_fusion), kind=kOutput, calls=%fused_computation.11 | convolution fusion | flops 135266304 | bytes 3674112 | tf_op jit(solution)/shard_map/blrmg,mng->blrmn/dot_general | solution.py:47
  36.3 1.0 copy-done.8
  37.3 1.0 fusion.31
  38.3 1.9 %copy.32 = bf16[1,32,2,16,256]{1,2,3,0,4:T(2,128)(2,1)S(1)} copy(bf16[1,32,2,16,256]{4,1,2,3,0:T(8,128)(2,1)S(1)} %fusion.31) | data formatting | bytes 1048576 | tf_op jit(solution)/shard_map/convert_element_type | solution.py:51
  40.2 2.0 %reshape.163 = bf16[16,2,8192]{2,1,0:T(2,128)(2,1)S(1)} reshape(bf16[256,1,16,2,32]{4,3,2,1,0:T(2,128)(2,1)S(1)} %bitcast.127) | data formatting | bytes 1048576
  42.2 18.5 %all_to_all.60 = bf16[16,2,8192]{2,1,0:T(2,128)(2,1)} all-to-all(bf16[16,2,8192]{2,1,0:T(2,128)(2,1)S(1)} %reshape.163), channel_id=1, replica_groups=mesh['tile'=16,'pair'=2] {'tile'}, dimensions={0} | all-to-all | bytes 1048576 | tf_op jit(solution)/shard_map/all_to_all | solution.py:55
  60.7 5.1 %reshape.164 = bf16[256,1,16,2,32]{4,3,2,1,0:T(2,128)(2,1)S(1)} reshape(bf16[16,2,8192]{2,1,0:T(2,128)(2,1)} %all_to_all.60) | data formatting | bytes 1048576
  65.8 0.8 copy.33
  66.6 0.6 copy.34
  67.2 2.1 %copy.35 = bf16[32,2,256,16]{2,3,1,0:T(8,128)(2,1)S(1)} copy(bf16[32,2,256,16]{0,3,2,1:T(8,128)(2,1)S(1)} %bitcast.132) | data formatting | bytes 1048576 | tf_op jit(solution)/shard_map/reshape.11
  69.3 1.8 %fusion.39 = (bf16[1,32,16,512]{3,2,1,0:T(8,128)(2,1)S(1)}, f32[32,16,512]{2,1,0:T(8,128)S(1)}) fusion(bf16[1,32,16,512]{3,2,1,0:T(8,128)(2,1)} %param.7, bf16[1,32,16,512]{3,2,1,0:T(8,128)(2,1)} %param.5, bf16[32,2,256,16]{2,3,1,0:T(8,128)(2,1)S(1)} %copy.35, bf16[512,2,256]{2,0,1:T(8,128)(2,1)S(1)} %fusion.36), kind=kOutput, calls=%fused_computation.33 | convolution fusion | flops 269746176 | bytes 3670016 | tf_op jit(solution)/shard_map/blrmg,jrm->blgj/dot_general | solution.py:44
  71.1 1.6 collective-permute-start
  72.7 12.4 %collective-permute-done = bf16[1,32,16,512]{3,2,1,0:T(8,128)(2,1)S(1)} collective-permute-done((bf16[1,32,16,512]{3,2,1,0:T(8,128)(2,1)S(1)}, bf16[1,32,16,512]{3,2,1,0:T(8,128)(2,1)S(1)}, u32[]{:S(2)}, u32[]{:S(2)}) %collective-permute-start) | collective-permute-done | bytes 524320 | tf_op jit(solution)/shard_map/ppermute | solution.py:15
  85.0 0.7 fusion.51
  85.7 0.1 copy-done.4
  85.8 0.5 fusion.35
  86.3 3.0 %copy.37 = bf16[1,32,2,256,16]{1,4,2,0,3:T(8,128)(2,1)S(1)} copy(bf16[1,32,2,256,16]{3,1,4,2,0:T(8,128)(2,1)S(1)} %fusion.35) | data formatting | bytes 1048576 | tf_op jit(solution)/shard_map/convert_element_type | solution.py:41
  89.3 2.0 %reshape.165 = bf16[16,2,8192]{2,1,0:T(2,128)(2,1)S(1)} reshape(bf16[256,1,2,16,32]{4,3,2,1,0:T(8,128)(2,1)S(1)} %bitcast.128) | data formatting | bytes 1048576
  91.3 18.8 %all_to_all.61 = bf16[16,2,8192]{2,1,0:T(2,128)(2,1)} all-to-all(bf16[16,2,8192]{2,1,0:T(2,128)(2,1)S(1)} %reshape.165), channel_id=1, replica_groups=mesh['tile'=16,'pair'=2] {'tile'}, dimensions={0} | all-to-all | bytes 1048576 | tf_op jit(solution)/shard_map/all_to_all | solution.py:58
  110.0 3.1 %reshape.166 = bf16[256,1,2,16,32]{4,3,2,1,0:T(8,128)(2,1)S(1)} reshape(bf16[16,2,8192]{2,1,0:T(2,128)(2,1)} %all_to_all.61) | data formatting | bytes 1048576
  113.1 0.4 copy.38
  113.5 0.6 copy.39
  114.0 1.0 copy-done.6
  115.1 0.3 copy-done.9
  115.3 2.6 %multiply_reduce_fusion = (f32[32,256]{1,0:T(8,128)S(1)}, f32[1,32,2,16,256]{4,1,2,3,0:T(8,128)S(1)}) fusion(f32[1,32,2,16,256]{4,1,2,3,0:T(8,128)S(1)} %copy-done.9, bf16[32,2,16,256]{0,3,2,1:T(8,128)(2,1)S(1)} %bitcast.140, bf16[16,256,256]{2,1,0:T(8,128)(2,1)S(1)} %copy-done.6, pred[16,256]{1,0:T(8,128)(4,1)S(1)} %iota_compare_fusion), kind=kOutput, calls=%fused_computation.34 | convolution fusion | flops 135782400 | bytes 4755456 | tf_op jit(solution)/shard_map/blrmg,mng->blrmn/dot_general | solution.py:47
  117.9 1.1 fusion.28
  119.0 1.9 %copy.41 = bf16[1,32,2,16,256]{1,2,3,0,4:T(2,128)(2,1)S(1)} copy(bf16[1,32,2,16,256]{4,1,2,3,0:T(8,128)(2,1)S(1)} %fusion.28) | data formatting | bytes 1048576 | tf_op jit(solution)/shard_map/convert_element_type | solution.py:51
  120.9 2.7 %reshape.167 = bf16[16,2,8192]{2,1,0:T(2,128)(2,1)} reshape(bf16[256,1,16,2,32]{4,3,2,1,0:T(2,128)(2,1)S(1)} %bitcast.129) | data formatting | bytes 1048576
  123.6 4.1 %all-to-all-start.3 = ((bf16[16,2,8192]{2,1,0:T(2,128)(2,1)}), bf16[16,2,8192]{2,1,0:T(2,128)(2,1)S(1)}, u32[]{:S(2)}, u32[]{:S(2)}) async-start(bf16[16,2,8192]{2,1,0:T(2,128)(2,1)} %reshape.167), calls=%async_computation.3 | async-start | bytes 1048576 | tf_op jit(solution)/shard_map/all_to_all | solution.py:55
  127.7 41.0 %psum.7 = f32[32,256]{1,0:T(8,128)S(1)} all-reduce(f32[32,256]{1,0:T(8,128)S(1)} %get-tuple-element.4), channel_id=1, replica_groups=mesh['tile'=16,'pair'=2] {'tile','pair'}, use_global_device_ids=true, to_apply=%region_1.2 | all-reduce | flops 8192 | bytes 65536 | tf_op jit(solution)/shard_map/psum | solution.py:77
  168.6 0.6 broadcast_multiply_fusion
  169.2 1.0 reshape.168
  170.3 0.8 copy.42
  171.1 0.6 copy.43
  171.7 3.0 %copy.44 = bf16[32,2,256,16]{2,3,1,0:T(8,128)(2,1)} copy(bf16[32,2,256,16]{0,3,2,1:T(8,128)(2,1)S(1)} %bitcast.135) | data formatting | bytes 1048576 | tf_op jit(solution)/shard_map/reshape.20
  174.6 3.2 %fusion.20 = f32[1,32,16,512]{3,2,1,0:T(8,128)} fusion(bf16[32,2,256,16]{2,3,1,0:T(8,128)(2,1)} %copy.44, bf16[512,2,256]{2,0,1:T(8,128)(2,1)S(1)} %fusion.36, bf16[1,32,16,512]{3,2,1,0:T(8,128)(2,1)} %copy-done.4, bf16[1,32,16,512]{3,2,1,0:T(8,128)(2,1)} %param.6, bf16[1,32,16,512]{3,2,1,0:T(8,128)(2,1)S(1)} %copy-done.1), kind=kOutput, calls=%fused_computation.14 | convolution fusion | flops 272367616 | bytes 3670016 | tf_op jit(solution)/shard_map/blrmg,jrm->blgj/dot_general | solution.py:44
  (17 shorter events, 0.0 us)
Async XLA Ops:
  0.6 2.2 %copy-start.2 = (bf16[1,32,16,512]{3,2,1,0:T(8,128)(2,1)S(1)}, bf16[1,32,16,512]{3,2,1,0:T(8,128)(2,1)}, u32[]{:S(2)}) copy-start(bf16[1,32,16,512]{3,2,1,0:T(8,128)(2,1)} %param.5) | copy-start | bytes 1572868
  9.0 21.9 %all-to-all-start = ((bf16[16,2,8192]{2,1,0:T(2,128)(2,1)}), bf16[16,2,8192]{2,1,0:T(2,128)(2,1)S(1)}, u32[]{:S(2)}, u32[]{:S(2)}) async-start(bf16[16,2,8192]{2,1,0:T(2,128)(2,1)} %reshape.161), calls=%async_computation | async-start | bytes 1048576 | tf_op jit(solution)/shard_map/all_to_all | solution.py:58
  32.2 1.6 copy-start.5
  33.8 3.5 %copy-start.7 = (f32[32,256]{1,0:T(8,128)S(1)}, f32[32,256]{1,0:T(8,128)}, u32[]{:S(2)}) copy-start(f32[32,256]{1,0:T(8,128)} %param.9) | copy-start | bytes 98308
  36.3 1.0 copy-start.8
  69.3 15.7 %copy-start.3 = (bf16[1,32,16,512]{3,2,1,0:T(8,128)(2,1)S(1)}, bf16[1,32,16,512]{3,2,1,0:T(8,128)(2,1)}, u32[]{:S(2)}) copy-start(bf16[1,32,16,512]{3,2,1,0:T(8,128)(2,1)} %param.6) | copy-start | bytes 1572868
  71.1 14.6 %copy-start = (bf16[1,32,16,512]{3,2,1,0:T(8,128)(2,1)}, bf16[1,32,16,512]{3,2,1,0:T(8,128)(2,1)S(1)}, u32[]{:S(2)}) copy-start(bf16[1,32,16,512]{3,2,1,0:T(8,128)(2,1)S(1)} %get-tuple-element.2) | copy-start | bytes 1572868
  71.1 13.9 %collective-permute-start = (bf16[1,32,16,512]{3,2,1,0:T(8,128)(2,1)S(1)}, bf16[1,32,16,512]{3,2,1,0:T(8,128)(2,1)S(1)}, u32[]{:S(2)}, u32[]{:S(2)}) collective-permute-start(bf16[1,32,16,512]{3,2,1,0:T(8,128)(2,1)S(1)} %get-tuple-element.2), channel_id=1, source_target_pairs={{0,1},{1,0},{2,3},{3,2},{4,5},{5,4},{6,7},{7,6},{8,9},{9,8},{10,11... | collective-permute-start | bytes 1572872 | tf_op jit(solution)/shard_map/ppermute | solution.py:15
  85.0 0.8 copy-start.4
  113.5 1.6 copy-start.6
  113.5 1.8 %copy-start.9 = (f32[1,32,2,16,256]{4,1,2,3,0:T(8,128)S(1)}, f32[1,32,2,16,256]{4,1,2,3,0:T(8,128)}, u32[]{:S(2)}) copy-start(f32[1,32,2,16,256]{4,1,2,3,0:T(8,128)} %copy-done.8) | copy-start | bytes 3145732
  123.6 45.7 %all-to-all-start.3 = ((bf16[16,2,8192]{2,1,0:T(2,128)(2,1)}), bf16[16,2,8192]{2,1,0:T(2,128)(2,1)S(1)}, u32[]{:S(2)}, u32[]{:S(2)}) async-start(bf16[16,2,8192]{2,1,0:T(2,128)(2,1)} %reshape.167), calls=%async_computation.3 | async-start | bytes 1048576 | tf_op jit(solution)/shard_map/all_to_all | solution.py:55
  171.7 3.0 %copy-start.1 = (bf16[1,32,16,512]{3,2,1,0:T(8,128)(2,1)S(1)}, bf16[1,32,16,512]{3,2,1,0:T(8,128)(2,1)}, u32[]{:S(2)}) copy-start(bf16[1,32,16,512]{3,2,1,0:T(8,128)(2,1)} %copy-done) | copy-start | bytes 1572868
where the time goes:
time: 178 us
  blocking collectives  78.2 us (44%)
  local copies, waits for them, and re-layouts  42.3 us (24%)
  waiting for transfers between devices  26.7 us (15%)
  matrix products  13.1 us (7%)
  starting transfers between devices  13 us (7%)
  other arithmetic  3.55 us (2%)
    psum x1, blocking collectives, body(): total = lax.psum(partial_sum, ('tile', 'pair'))  41 us
    unnamed x28, local copies, waits for them, and re-layouts  22.8 us
    all_to_all x1, blocking collectives, spectral(): lax.all_to_all(grid_coef, 'tile', split_axis=3, concat_axis=4, tiled=True)  18.8 us
    all_to_all x1, blocking collectives, to_grid(): return lax.all_to_all(back, 'tile', split_axis=4, concat_axis=3, tiled=True)  18.5 us
    all_to_all x1, waiting for transfers between devices, spectral(): lax.all_to_all(grid_coef, 'tile', split_axis=3, concat_axis=4, tiled=True)  14.4 us
    ppermute x1, waiting for transfers between devices, swapped(): return lax.ppermute(value, axis, pairs)  12.4 us
    all_to_all x1, starting transfers between devices, spectral(): lax.all_to_all(grid_coef, 'tile', split_axis=3, concat_axis=4, tiled=True)  7.38 us
    convert_element_type x2, local copies, waits for them, and re-layouts, analyse(): return jnp.einsum('blgj,jrm->blrmg', grid, table, preferred_element_type=...  6.01 us
  transfers between devices with their start and end apart: 3, of which 2 were waited for; matrix products, arithmetic and copies ran while one was open for 0% of the time, Pallas kernels for 0%

commit v1 on v0

--- a/solution.py
+++ b/solution.py
@@ -1,8 +1,13 @@
+import functools
 import math
 
 import jax
 import jax.numpy as jnp
+import ml_dtypes
+import numpy as np
 from jax import lax
+from jax.experimental import pallas as pl
+from jax.experimental.pallas import tpu as pltpu
 from jax.sharding import PartitionSpec as P
 
 NLON = 512
@@ -79,6 +84,371 @@
     return (grad_state, total * (members * M) ** (-0.5))
 
 
+MESH = pl.DeviceIdType.MESH
+BF16, F32 = jnp.bfloat16, jnp.float32
+SIDE = 16
+CHUNKS = 2
+
+
+def table_rows(length, waves):
+    points = np.arange(length)
+    orders = np.arange(waves)
+    angle = (points[:, None] * orders[None, :] % length) * (2.0 * math.pi / length)
+    both = np.stack([np.cos(angle), -np.sin(angle)], axis=0) * length ** (-0.5)
+    split = both.reshape(2, length, waves // SIDE, 2, 8)
+    return split.transpose(4, 0, 2, 3, 1).reshape(2 * waves, length).astype(ml_dtypes.bfloat16)
+
+
+def exchanged(parts):
+    lane = lax.broadcasted_iota(jnp.int32, parts[0].shape, 1)
+    parts = list(parts)
+    for bit in (1, 2, 4, 8):
+        high = (lane & bit) != 0
+        for i in range(16):
+            if not i & bit:
+                a, b = parts[i], parts[i | bit]
+                parts[i] = jnp.where(high, pltpu.roll(b, bit, 1), a)
+                parts[i | bit] = jnp.where(high, b, pltpu.roll(a, 128 - bit, 1))
+    return parts
+
+
+def kernel(
+    tiles, pairs, levels,
+    state, table, damp, target_hbm, pert_hbm, leg_hbm,
+    out, total,
+    target, pert, leg, mk_n, mk_g, rhs, gain, coefs, dacc, bents, adv, other, gw, wave,
+    four, turned, send, recv, rs_src, rs_recv, ag_src, ag_recv,
+    load_sem, send_sem, recv_sem, psend_sem, precv_sem, rs_sem, ag_sem,
+):
+    me, mine = lax.axis_index("tile"), lax.axis_index("pair")
+    flat = mine * tiles + me
+    count = tiles * pairs
+    lev = levels // CHUNKS
+    blocks = lev // 8
+    rows = lev * SIDE
+    width = blocks * 128
+    buddy = mine + 1 - 2 * lax.rem(mine, 2)
+
+    loads = [
+        pltpu.make_async_copy(src, dst, load_sem.at[i])
+        for i, (src, dst) in enumerate(((leg_hbm, leg), (pert_hbm, pert), (target_hbm, target)))
+    ]
+    for load in loads:
+        load.start()
+
+    barrier = pltpu.get_barrier_semaphore()
+
+    def greet(step, _):
+        to = lax.rem(flat + step, count)
+        pl.semaphore_signal(
+            barrier, inc=1,
+            device_id={"tile": lax.rem(to, tiles), "pair": to // tiles}, device_id_type=MESH,
+        )
+        return 0
+
+    lax.fori_loop(1, count, greet, 0)
+
+    def all_to_all(slot):
+        def one(step, _):
+            to = lax.rem(me + step, tiles)
+            pltpu.make_async_remote_copy(
+                src_ref=send.at[slot, to], dst_ref=recv.at[slot, me],
+                send_sem=send_sem.at[slot], recv_sem=recv_sem.at[slot],
+                device_id={"tile": to}, device_id_type=MESH,
+            ).start()
+            return 0
+
+        lax.fori_loop(1, tiles, one, 0)
+        pltpu.make_async_copy(send.at[slot, me], recv.at[slot, me], recv_sem.at[slot]).start()
+
+    def arrived(slot):
+        pltpu.make_async_copy(recv.at[slot], recv.at[slot], recv_sem.at[slot]).wait()
+
+    def analyse(slot, grid):
+        four[...] = lax.dot_general(
+            table[...], grid, (((1,), (1,)), ((), ())), preferred_element_type=F32
+        )
+        for b in range(blocks):
+            lanes = pl.ds(b * 128, 128)
+
+            def turn(ro, _):
+                at = pl.multiple_of(ro * 8, 8)
+                parts = exchanged([four[pl.ds(c * 32 + at, 8), lanes] for c in range(16)])
+                for g in range(16):
+                    turned[pl.ds(g * 32 + at, 8), :] = parts[g]
+                return 0
+
+            lax.fori_loop(0, 4, turn, 0)
+            for row in range(32):
+                send[slot, row // 2, (row % 2) * blocks + b] = turned[
+                    pl.ds(row, 16, stride=32), :
+                ].astype(BF16)
+
+    def synthesise(slot):
+        for b in range(blocks):
+            lanes = pl.ds(b * 128, 128)
+            for row in range(32):
+                turned[pl.ds(row * 16, 16), :] = recv[
+                    slot, row // 2, (row % 2) * blocks + b
+                ].astype(F32)
+
+            def turn(ro, _):
+                at = pl.multiple_of(ro * 8, 8)
+                parts = exchanged(
+                    [turned[pl.ds(at * 16 + g, 8, stride=16), :] for g in range(16)]
+                )
+                for c in range(16):
+                    four[pl.ds(c * 32 + at, 8), lanes] = parts[c]
+                return 0
+
+            lax.fori_loop(0, 4, turn, 0)
+        wave[...] = lax.dot_general(
+            four[...].astype(BF16), table[...], (((0,), (0,)), ((), ())),
+            preferred_element_type=F32,
+        )
+
+    lane_m = lax.rem(lax.broadcasted_iota(jnp.int32, (SIDE * 16, width), 1), 16) // 2
+
+    def spread(value):
+        for m in range(8):
+            rhs[pl.ds(m * 256, 256), :] = jnp.where(lane_m == m, value, 0.0).astype(BF16)
+
+    def spectral(ch, slot_in, slot_out, backward):
+        for hi in range(2):
+            held = [
+                recv[slot_in, :, hi * blocks + b].reshape(SIDE * SIDE, 128).astype(F32)
+                for b in range(blocks)
+            ]
+            spread(jnp.concatenate(held, axis=1))
+            coef = jnp.dot(mk_n[hi], rhs[...], preferred_element_type=F32)
+            if backward:
+                product = coefs[ch, hi] * coef
+                dacc[ch] = product if hi == 0 else dacc[ch] + product
+            else:
+                coefs[ch, hi] = coef
+            spread(coef * gain[ch])
+            back = jnp.dot(mk_g[hi], rhs[...], preferred_element_type=F32).astype(BF16)
+            for b in range(blocks):
+                send[slot_out, :, hi * blocks + b] = back[:, b * 128 : b * 128 + 128].reshape(
+                    SIDE, SIDE, 128
+                )
+
+    def pick(ch):
+        level = lax.broadcasted_iota(jnp.int32, (levels, width), 0)
+        lane = lax.broadcasted_iota(jnp.int32, (levels, width), 1)
+        return (level == ch * lev + lane // 16).astype(F32)
+
+    def exchange(ch):
+        return pltpu.make_async_remote_copy(
+            src_ref=adv.at[ch], dst_ref=other.at[ch],
+            send_sem=psend_sem.at[ch], recv_sem=precv_sem.at[ch],
+            device_id={"pair": buddy}, device_id_type=MESH,
+        )
+
+    for ch in range(CHUNKS):
+        analyse(ch, state[pl.ds(ch * rows, rows), :])
+        if ch == 0:
+            pl.semaphore_wait(barrier, count - 1)
+        all_to_all(ch)
+
+    loads[0].wait()
+    for i in range(16):
+        degree = lax.broadcasted_iota(jnp.int32, (256, 256), 0)
+        own = jnp.where(degree >= me * SIDE + i, leg[i].astype(F32), 0.0)
+        at = pl.ds((i % 8) * 256, 256)
+        mk_n[i // 8, :, at] = own.astype(BF16)
+        mk_g[i // 8, :, at] = own.T.astype(BF16)
+    for ch in range(CHUNKS):
+        gain[ch] = lax.dot_general(
+            damp[...], pick(ch), (((0,), (0,)), ((), ())),
+            precision=lax.Precision.HIGHEST, preferred_element_type=F32,
+        )
+    loads[1].wait()
+    loads[2].wait()
+
+    for ch in range(CHUNKS):
+        arrived(ch)
+        spectral(ch, ch, CHUNKS + ch, False)
+        all_to_all(CHUNKS + ch)
+
+    for ch in range(CHUNKS):
+        arrived(CHUNKS + ch)
+        synthesise(CHUNKS + ch)
+
+        def advance(step, _):
+            at = pl.ds(pl.multiple_of(step * 16, 16), 16)
+            all_at = pl.ds(pl.multiple_of(ch * rows + step * 16, 16), 16)
+            bent = jnp.tanh(wave[at, :])
+            bents[all_at, :] = bent
+            adv[ch, at, :] = (
+                state[all_at, :].astype(F32) + bent + pert[all_at, :].astype(F32)
+            ).astype(BF16)
+            return 0
+
+        lax.fori_loop(0, rows // 16, advance, 0)
+        exchange(ch).start()
+
+    for ch in range(CHUNKS):
+        exchange(ch).wait_recv()
+
+        def gradient(step, _):
+            at = pl.ds(pl.multiple_of(step * 16, 16), 16)
+            all_at = pl.ds(pl.multiple_of(ch * rows + step * 16, 16), 16)
+            own = adv[ch, at, :].astype(F32)
+            miss = own - target[all_at, :].astype(F32)
+            apart = own - other[ch, at, :].astype(F32)
+            grad_adv = 0.5 * miss * lax.rsqrt(miss * miss + 1.0) - 0.25 * apart * lax.rsqrt(
+                apart * apart + 1.0
+            )
+            bent = bents[all_at, :]
+            out[all_at, :] = grad_adv
+            gw[at, :] = (grad_adv * (1.0 - bent * bent)).astype(BF16)
+            return 0
+
+        lax.fori_loop(0, rows // 16, gradient, 0)
+        analyse(2 * CHUNKS + ch, gw[...])
+        all_to_all(2 * CHUNKS + ch)
+
+    for ch in range(CHUNKS):
+        arrived(2 * CHUNKS + ch)
+        spectral(ch, 2 * CHUNKS + ch, 3 * CHUNKS + ch, True)
+        all_to_all(3 * CHUNKS + ch)
+
+    partial = sum(
+        lax.dot_general(
+            pick(ch), dacc[ch], (((1,), (1,)), ((), ())),
+            precision=lax.Precision.HIGHEST, preferred_element_type=F32,
+        )
+        for ch in range(CHUNKS)
+    )
+    owners = levels // 8 * 2
+    for k in range(owners):
+        rs_src[k] = partial[k // 2 * 8 : k // 2 * 8 + 8, k % 2 * 128 : k % 2 * 128 + 128]
+
+    def rs_copy(k):
+        return pltpu.make_async_remote_copy(
+            src_ref=rs_src.at[k], dst_ref=rs_recv.at[flat],
+            send_sem=rs_sem.at[1 + k], recv_sem=rs_sem.at[0],
+            device_id={"tile": 2 * k, "pair": k % pairs}, device_id_type=MESH,
+        )
+
+    for k in range(owners):
+        is_owner = flat == (k % pairs) * tiles + 2 * k
+
+        @pl.when(jnp.logical_not(is_owner))
+        def _():
+            rs_copy(k).start()
+
+        @pl.when(is_owner)
+        def _():
+            pltpu.make_async_copy(rs_src.at[k], rs_recv.at[flat], rs_sem.at[0]).start()
+
+    block = me // 2
+    owns = jnp.logical_and(lax.rem(me, 2) == 0, lax.rem(block, pairs) == mine)
+
+    @pl.when(owns)
+    def _():
+        pltpu.make_async_copy(rs_recv, rs_recv, rs_sem.at[0]).wait()
+        ag_src[...] = jnp.sum(rs_recv[...], axis=0)
+
+        def one(step, _):
+            to = lax.rem(flat + step, count)
+            pltpu.make_async_remote_copy(
+                src_ref=ag_src, dst_ref=ag_recv.at[block],
+                send_sem=ag_sem.at[1], recv_sem=ag_sem.at[0],
+                device_id={"tile": lax.rem(to, tiles), "pair": to // tiles}, device_id_type=MESH,
+            ).start()
+            return 0
+
+        lax.fori_loop(1, count, one, 0)
+        pltpu.make_async_copy(ag_src, ag_recv.at[block], ag_sem.at[0]).start()
+
+    for ch in range(CHUNKS):
+        arrived(3 * CHUNKS + ch)
+        synthesise(3 * CHUNKS + ch)
+        at = pl.ds(ch * rows, rows)
+        out[at, :] = out[at, :] + wave[...]
+
+    pltpu.make_async_copy(ag_recv, ag_recv, ag_sem.at[0]).wait()
+    for k in range(owners):
+        total[k // 2 * 8 : k // 2 * 8 + 8, k % 2 * 128 : k % 2 * 128 + 128] = ag_recv[k] * (
+            (pairs * tiles * SIDE) ** (-0.5)
+        )
+
+    for slot in range(4 * CHUNKS):
+        gone = send.at[slot, pl.ds(0, tiles - 1)]
+        pltpu.make_async_copy(gone, gone, send_sem.at[slot]).wait()
+    for ch in range(CHUNKS):
+        exchange(ch).wait_send()
+    for k in range(owners):
+        @pl.when(flat != (k % pairs) * tiles + 2 * k)
+        def _():
+            rs_copy(k).wait_send()
+
+    @pl.when(owns)
+    def _():
+        gone = rs_recv.at[pl.ds(0, count - 1)]
+        pltpu.make_async_copy(gone, gone, ag_sem.at[1]).wait()
+
+
+def fused(tiles, pairs, state, target, perturbation, legendre, damp):
+    members, levels, lats, lons = state.shape
+    rows = levels * lats
+    part = rows // CHUNKS
+    width = levels // CHUNKS // 8 * 128
+    blocks = width // 128 * 2
+    flatten = lambda x: x.reshape(rows, lons)
+    dma = pltpu.SemaphoreType.DMA
+    grads, total = pl.pallas_call(
+        functools.partial(kernel, tiles, pairs, levels),
+        out_shape=(
+            jax.ShapeDtypeStruct((rows, lons), F32),
+            jax.ShapeDtypeStruct(damp.shape, F32),
+        ),
+        in_specs=[pl.BlockSpec(memory_space=pltpu.VMEM)] * 3
+        + [pl.BlockSpec(memory_space=pl.ANY)] * 3,
+        out_specs=(pl.BlockSpec(memory_space=pltpu.VMEM),) * 2,
+        scratch_shapes=[
+            pltpu.VMEM((rows, lons), BF16),
+            pltpu.VMEM((rows, lons), BF16),
+            pltpu.VMEM(legendre.shape, BF16),
+            pltpu.VMEM((2, 256, 2048), BF16),
+            pltpu.VMEM((2, 256, 2048), BF16),
+            pltpu.VMEM((2048, width), BF16),
+            pltpu.VMEM((CHUNKS, 256, width), F32),
+            pltpu.VMEM((CHUNKS, 2, 256, width), F32),
+            pltpu.VMEM((CHUNKS, 256, width), F32),
+            pltpu.VMEM((rows, lons), F32),
+            pltpu.VMEM((CHUNKS, part, lons), BF16),
+            pltpu.VMEM((CHUNKS, part, lons), BF16),
+            pltpu.VMEM((part, lons), BF16),
+            pltpu.VMEM((part, lons), F32),
+            pltpu.VMEM((512, width), F32),
+            pltpu.VMEM((512, 128), F32),
+            pltpu.VMEM((4 * CHUNKS, tiles, blocks, SIDE, 128), BF16),
+            pltpu.VMEM((4 * CHUNKS, tiles, blocks, SIDE, 128), BF16),
+            pltpu.VMEM((8, 8, 128), F32),
+            pltpu.VMEM((tiles * pairs, 8, 128), F32),
+            pltpu.VMEM((8, 128), F32),
+            pltpu.VMEM((8, 8, 128), F32),
+            dma((3,)),
+            dma((4 * CHUNKS,)),
+            dma((4 * CHUNKS,)),
+            dma((CHUNKS,)),
+            dma((CHUNKS,)),
+            dma((9,)),
+            dma((2,)),
+        ],
+        compiler_params=pltpu.CompilerParams(
+            collective_id=0, has_side_effects=True, vmem_limit_bytes=48 * 2**20
+        ),
+    )(
+        flatten(state), jnp.asarray(table_rows(NLON, M)), damp,
+        flatten(target), flatten(perturbation), legendre,
+    )
+    return grads.reshape(state.shape), total
+
+
 def solution(mesh):
     placed = (
         P("pair", None, "tile", None),
@@ -87,8 +457,17 @@
         P("tile", None, None),
         P(),
     )
+    tiles, pairs = mesh.shape["tile"], mesh.shape["pair"]
+
+    def local(state, target, perturbation, legendre, damp):
+        held = (state.shape, legendre.shape, damp.shape)
+        small = ((1, 32, SIDE, NLON), (SIDE, 256, 256), (32, 256))
+        if tiles == SIDE and pairs == 2 and held == small:
+            return fused(tiles, pairs, state, target, perturbation, legendre, damp)
+        return body(state, target, perturbation, legendre, damp)
+
     return jax.shard_map(
-        body,
+        local,
         mesh=mesh,
         in_specs=placed,
         out_specs=(P("pair", None, "tile", None), P()),

time: 178 us -> 83.6 us (0.47)
  blocking collectives: 78.2 us -> 0 us
  Pallas kernels: 0 us -> 74.4 us
  local copies, waits for them, and re-layouts: 42.3 us -> 8.09 us
  waiting for transfers between devices: 26.7 us -> 0 us
  matrix products: 13.1 us -> 0 us
  starting transfers between devices: 13 us -> 0 us
  other arithmetic: 3.55 us -> 0 us
    pallas_call x0 -> x1, Pallas kernels: none -> 74.4 us  [fused(): pl.pallas_call(functools.partial(kernel, tiles, pairs, levels), out_shape...]
    psum x1 -> x0, blocking collectives: 41 us -> none  [body(): total = lax.psum(partial_sum, ('tile', 'pair'))]
    all_to_all x2 -> x0, blocking collectives: 37.2 us -> none  [the longest x1 18.8 us: spectral(): lax.all_to_all(grid_coef, 'tile', split_axis=3, concat_axis=4, tiled=True)]
    unnamed x28 -> x14, local copies, waits for them, and re-layouts: 22.8 us -> 8.09 us
    all_to_all x2 -> x0, waiting for transfers between devices: 14.4 us -> none  [the longest x1 14.4 us: spectral(): lax.all_to_all(grid_coef, 'tile', split_axis=3, concat_axis=4, tiled=True)]
    dot_general x8 -> x0, matrix products: 13.1 us -> none  [the longest x2 5.12 us: spectral_pass(): jnp.einsum('blrmg,mng->blrmn', piece, masked, preferred_element_type=jnp....]
    ppermute x1 -> x0, waiting for transfers between devices: 12.4 us -> none  [swapped(): return lax.ppermute(value, axis, pairs)]
    all_to_all x2 -> x0, starting transfers between devices: 11.5 us -> none  [the longest x1 7.38 us: spectral(): lax.all_to_all(grid_coef, 'tile', split_axis=3, concat_axis=4, tiled=True)]
  transfers between devices with their start and end apart: 3 -> 0, of which waited for: 2 -> 0; matrix products, arithmetic and copies ran while one was open for 0% -> 0% of each run, Pallas kernels for 0% -> 0%
where the time goes in v1:
time: 83.6 us; the launch traced here: 83.2 us
  Pallas kernels  74.4 us (89%)
  local copies, waits for them, and re-layouts  8.09 us (10%)
    pallas_call x1, Pallas kernels, fused(): pl.pallas_call(functools.partial(kernel, tiles, pairs, levels), out_shape...  74.4 us
    unnamed x14, local copies, waits for them, and re-layouts  8.09 us

profile of v1, /device:TPU:0, one launch (start us, length us, event | category | flops | bytes accessed | tf_op | source)
XLA Modules:
  0.0 83.2 jit_solution(11481282297844594190)
XLA Ops:
  0.6 0.0 copy-start
  0.6 1.6 %copy-done = bf16[16,256,256]{2,1,0:T(8,128)(2,1)S(1)} copy-done((bf16[16,256,256]{2,1,0:T(8,128)(2,1)S(1)}, bf16[16,256,256]{2,1,0:T(8,128)(2,1)}, u32[]{:S(2)}) %copy-start) | copy-done | bytes 2097176
  2.2 0.0 copy-start.1
  2.2 1.0 %copy-done.1 = bf16[1,32,16,512]{3,2,1,0:T(8,128)(2,1)S(1)} copy-done((bf16[1,32,16,512]{3,2,1,0:T(8,128)(2,1)S(1)}, bf16[1,32,16,512]{3,2,1,0:T(8,128)(2,1)}, u32[]{:S(2)}) %copy-start.1) | copy-done | bytes 524312
  3.3 0.0 copy-start.2
  3.3 1.0 %copy-done.2 = bf16[1,32,16,512]{3,2,1,0:T(8,128)(2,1)S(1)} copy-done((bf16[1,32,16,512]{3,2,1,0:T(8,128)(2,1)S(1)}, bf16[1,32,16,512]{3,2,1,0:T(8,128)(2,1)}, u32[]{:S(2)}) %copy-start.2) | copy-done | bytes 524312
  4.3 0.0 copy-start.3
  4.3 1.0 %copy-done.3 = bf16[1,32,16,512]{3,2,1,0:T(8,128)(2,1)S(1)} copy-done((bf16[1,32,16,512]{3,2,1,0:T(8,128)(2,1)S(1)}, bf16[1,32,16,512]{3,2,1,0:T(8,128)(2,1)}, u32[]{:S(2)}) %copy-start.3) | copy-done | bytes 524312
  5.3 0.0 copy-start.4
  5.4 1.0 %copy-done.4 = bf16[512,512]{1,0:T(8,128)(2,1)S(1)} copy-done((bf16[512,512]{1,0:T(8,128)(2,1)S(1)}, bf16[512,512]{1,0:T(8,128)(2,1)}, u32[]{:S(2)}) %copy-start.4) | copy-done | bytes 524312
  6.4 0.0 copy-start.5
  6.4 0.8 copy-done.5
  7.2 74.4 %shard_map.77 = (f32[512,512]{1,0:T(8,128)S(1)}, f32[32,256]{1,0:T(8,128)S(1)}) custom-call(bf16[512,512]{1,0:T(8,128)(2,1)S(1)} %bitcast.5, bf16[512,512]{1,0:T(8,128)(2,1)S(1)} %copy-done.4, f32[32,256]{1,0:T(8,128)S(1)} %copy-done.5, bf16[512,512]{1,0:T(8,128)(2,1)S(1)} %bitcast.6, bf16[512,512]{1,0:T(8,128)(2,1)S(1)} %bitcast.7, ...), custom_call_target="tpu_custom_call" | custom-call | tf_op jit(solution)/shard_map/pallas_call | solution.py:402
  81.6 1.0 %copy.10 = f32[1,32,16,512]{3,2,1,0:T(8,128)} copy(f32[1,32,16,512]{3,2,1,0:T(8,128)S(1)} %bitcast.4) | data formatting | bytes 2097152
  82.6 0.6 copy.11
Async XLA Ops:
  0.6 1.6 %copy-start = (bf16[16,256,256]{2,1,0:T(8,128)(2,1)S(1)}, bf16[16,256,256]{2,1,0:T(8,128)(2,1)}, u32[]{:S(2)}) copy-start(bf16[16,256,256]{2,1,0:T(8,128)(2,1)} %leg_hbm.1) | copy-start | bytes 6291460
  2.2 1.0 %copy-start.1 = (bf16[1,32,16,512]{3,2,1,0:T(8,128)(2,1)S(1)}, bf16[1,32,16,512]{3,2,1,0:T(8,128)(2,1)}, u32[]{:S(2)}) copy-start(bf16[1,32,16,512]{3,2,1,0:T(8,128)(2,1)} %param.6) | copy-start | bytes 1572868
  3.3 1.0 %copy-start.2 = (bf16[1,32,16,512]{3,2,1,0:T(8,128)(2,1)S(1)}, bf16[1,32,16,512]{3,2,1,0:T(8,128)(2,1)}, u32[]{:S(2)}) copy-start(bf16[1,32,16,512]{3,2,1,0:T(8,128)(2,1)} %param.7) | copy-start | bytes 1572868
  4.3 1.0 %copy-start.3 = (bf16[1,32,16,512]{3,2,1,0:T(8,128)(2,1)S(1)}, bf16[1,32,16,512]{3,2,1,0:T(8,128)(2,1)}, u32[]{:S(2)}) copy-start(bf16[1,32,16,512]{3,2,1,0:T(8,128)(2,1)} %param.8) | copy-start | bytes 1572868
  5.3 1.0 %copy-start.4 = (bf16[512,512]{1,0:T(8,128)(2,1)S(1)}, bf16[512,512]{1,0:T(8,128)(2,1)}, u32[]{:S(2)}) copy-start(bf16[512,512]{1,0:T(8,128)(2,1)} %constant.2.clone.table) | copy-start | bytes 1572868
  6.4 0.8 copy-start.5

commit v2 on v1

--- a/solution.py
+++ b/solution.py
@@ -87,7 +87,8 @@
 MESH = pl.DeviceIdType.MESH
 BF16, F32 = jnp.bfloat16, jnp.float32
 SIDE = 16
-CHUNKS = 2
+BLOCKS = 4
+STEP_OUT, STEP_IN = 40, 24
 
 
 def table_rows(length, waves):
@@ -123,10 +124,9 @@
     me, mine = lax.axis_index("tile"), lax.axis_index("pair")
     flat = mine * tiles + me
     count = tiles * pairs
-    lev = levels // CHUNKS
-    blocks = lev // 8
-    rows = lev * SIDE
-    width = blocks * 128
+    halves = BLOCKS // 2
+    rows = levels * SIDE // BLOCKS
+    width = 256
     buddy = mine + 1 - 2 * lax.rem(mine, 2)
 
     loads = [
@@ -168,40 +168,22 @@
         four[...] = lax.dot_general(
             table[...], grid, (((1,), (1,)), ((), ())), preferred_element_type=F32
         )
-        for b in range(blocks):
-            lanes = pl.ds(b * 128, 128)
-
-            def turn(ro, _):
-                at = pl.multiple_of(ro * 8, 8)
-                parts = exchanged([four[pl.ds(c * 32 + at, 8), lanes] for c in range(16)])
-                for g in range(16):
-                    turned[pl.ds(g * 32 + at, 8), :] = parts[g]
-                return 0
-
-            lax.fori_loop(0, 4, turn, 0)
-            for row in range(32):
-                send[slot, row // 2, (row % 2) * blocks + b] = turned[
-                    pl.ds(row, 16, stride=32), :
-                ].astype(BF16)
+        for at in range(0, 32, 8):
+            parts = exchanged([four[c * 32 + at : c * 32 + at + 8, :] for c in range(16)])
+            for g in range(16):
+                turned[pl.ds(g * STEP_OUT + at, 8), :] = parts[g]
+        for row in range(32):
+            send[slot, row // 2, row % 2] = turned[pl.ds(row, 16, stride=STEP_OUT), :].astype(BF16)
 
     def synthesise(slot):
-        for b in range(blocks):
-            lanes = pl.ds(b * 128, 128)
-            for row in range(32):
-                turned[pl.ds(row * 16, 16), :] = recv[
-                    slot, row // 2, (row % 2) * blocks + b
-                ].astype(F32)
-
-            def turn(ro, _):
-                at = pl.multiple_of(ro * 8, 8)
-                parts = exchanged(
-                    [turned[pl.ds(at * 16 + g, 8, stride=16), :] for g in range(16)]
-                )
-                for c in range(16):
-                    four[pl.ds(c * 32 + at, 8), lanes] = parts[c]
-                return 0
-
-            lax.fori_loop(0, 4, turn, 0)
+        for row in range(32):
+            turned[pl.ds(row * STEP_IN, 16), :] = recv[slot, row // 2, row % 2].astype(F32)
+        for at in range(0, 32, 8):
+            parts = exchanged(
+                [turned[pl.ds(at * STEP_IN + g, 8, stride=STEP_IN), :] for g in range(16)]
+            )
+            for c in range(16):
+                four[c * 32 + at : c * 32 + at + 8, :] = parts[c]
         wave[...] = lax.dot_general(
             four[...].astype(BF16), table[...], (((0,), (0,)), ((), ())),
             preferred_element_type=F32,
@@ -213,30 +195,30 @@
         for m in range(8):
             rhs[pl.ds(m * 256, 256), :] = jnp.where(lane_m == m, value, 0.0).astype(BF16)
 
-    def spectral(ch, slot_in, slot_out, backward):
+    def spectral(half, phase, backward):
+        first = phase * BLOCKS + 2 * half
         for hi in range(2):
             held = [
-                recv[slot_in, :, hi * blocks + b].reshape(SIDE * SIDE, 128).astype(F32)
-                for b in range(blocks)
+                recv[first + b, :, hi].reshape(SIDE * SIDE, 128).astype(F32) for b in range(2)
             ]
             spread(jnp.concatenate(held, axis=1))
             coef = jnp.dot(mk_n[hi], rhs[...], preferred_element_type=F32)
             if backward:
-                product = coefs[ch, hi] * coef
-                dacc[ch] = product if hi == 0 else dacc[ch] + product
+                product = coefs[half, hi] * coef
+                dacc[half] = product if hi == 0 else dacc[half] + product
             else:
-                coefs[ch, hi] = coef
-            spread(coef * gain[ch])
+                coefs[half, hi] = coef
+            spread(coef * gain[half])
             back = jnp.dot(mk_g[hi], rhs[...], preferred_element_type=F32).astype(BF16)
-            for b in range(blocks):
-                send[slot_out, :, hi * blocks + b] = back[:, b * 128 : b * 128 + 128].reshape(
+            for b in range(2):
+                send[first + BLOCKS + b, :, hi] = back[:, b * 128 : b * 128 + 128].reshape(
                     SIDE, SIDE, 128
                 )
 
-    def pick(ch):
+    def pick(half):
         level = lax.broadcasted_iota(jnp.int32, (levels, width), 0)
         lane = lax.broadcasted_iota(jnp.int32, (levels, width), 1)
-        return (level == ch * lev + lane // 16).astype(F32)
+        return (level == half * 16 + lane // 16).astype(F32)
 
     def exchange(ch):
         return pltpu.make_async_remote_copy(
@@ -245,7 +227,7 @@
             device_id={"pair": buddy}, device_id_type=MESH,
         )
 
-    for ch in range(CHUNKS):
+    for ch in range(BLOCKS):
         analyse(ch, state[pl.ds(ch * rows, rows), :])
         if ch == 0:
             pl.semaphore_wait(barrier, count - 1)
@@ -258,7 +240,7 @@
         at = pl.ds((i % 8) * 256, 256)
         mk_n[i // 8, :, at] = own.astype(BF16)
         mk_g[i // 8, :, at] = own.T.astype(BF16)
-    for ch in range(CHUNKS):
+    for ch in range(halves):
         gain[ch] = lax.dot_general(
             damp[...], pick(ch), (((0,), (0,)), ((), ())),
             precision=lax.Precision.HIGHEST, preferred_element_type=F32,
@@ -266,14 +248,19 @@
     loads[1].wait()
     loads[2].wait()
 
-    for ch in range(CHUNKS):
-        arrived(ch)
-        spectral(ch, ch, CHUNKS + ch, False)
-        all_to_all(CHUNKS + ch)
-
-    for ch in range(CHUNKS):
-        arrived(CHUNKS + ch)
-        synthesise(CHUNKS + ch)
+    def through(phase, backward):
+        for half in range(halves):
+            for b in range(2):
+                arrived(phase * BLOCKS + 2 * half + b)
+            spectral(half, phase, backward)
+            for b in range(2):
+                all_to_all((phase + 1) * BLOCKS + 2 * half + b)
+
+    through(0, False)
+
+    def forward(ch):
+        arrived(BLOCKS + ch)
+        synthesise(BLOCKS + ch)
 
         def advance(step, _):
             at = pl.ds(pl.multiple_of(step * 16, 16), 16)
@@ -288,7 +275,7 @@
         lax.fori_loop(0, rows // 16, advance, 0)
         exchange(ch).start()
 
-    for ch in range(CHUNKS):
+    def reverse(ch):
         exchange(ch).wait_recv()
 
         def gradient(step, _):
@@ -306,20 +293,23 @@
             return 0
 
         lax.fori_loop(0, rows // 16, gradient, 0)
-        analyse(2 * CHUNKS + ch, gw[...])
-        all_to_all(2 * CHUNKS + ch)
-
-    for ch in range(CHUNKS):
-        arrived(2 * CHUNKS + ch)
-        spectral(ch, 2 * CHUNKS + ch, 3 * CHUNKS + ch, True)
-        all_to_all(3 * CHUNKS + ch)
+        analyse(2 * BLOCKS + ch, gw[...])
+        all_to_all(2 * BLOCKS + ch)
+
+    forward(0)
+    for ch in range(1, BLOCKS):
+        forward(ch)
+        reverse(ch - 1)
+    reverse(BLOCKS - 1)
+
+    through(2, True)
 
     partial = sum(
         lax.dot_general(
             pick(ch), dacc[ch], (((1,), (1,)), ((), ())),
             precision=lax.Precision.HIGHEST, preferred_element_type=F32,
         )
-        for ch in range(CHUNKS)
+        for ch in range(halves)
     )
     owners = levels // 8 * 2
     for k in range(owners):
@@ -345,6 +335,14 @@
 
     block = me // 2
     owns = jnp.logical_and(lax.rem(me, 2) == 0, lax.rem(block, pairs) == mine)
+
+    def finish(ch):
+        arrived(3 * BLOCKS + ch)
+        synthesise(3 * BLOCKS + ch)
+        at = pl.ds(ch * rows, rows)
+        out[at, :] = out[at, :] + wave[...]
+
+    finish(0)
 
     @pl.when(owns)
     def _():
@@ -363,11 +361,8 @@
         lax.fori_loop(1, count, one, 0)
         pltpu.make_async_copy(ag_src, ag_recv.at[block], ag_sem.at[0]).start()
 
-    for ch in range(CHUNKS):
-        arrived(3 * CHUNKS + ch)
-        synthesise(3 * CHUNKS + ch)
-        at = pl.ds(ch * rows, rows)
-        out[at, :] = out[at, :] + wave[...]
+    for ch in range(1, BLOCKS):
+        finish(ch)
 
     pltpu.make_async_copy(ag_recv, ag_recv, ag_sem.at[0]).wait()
     for k in range(owners):
@@ -375,10 +370,10 @@
             (pairs * tiles * SIDE) ** (-0.5)
         )
 
-    for slot in range(4 * CHUNKS):
+    for slot in range(4 * BLOCKS):
         gone = send.at[slot, pl.ds(0, tiles - 1)]
         pltpu.make_async_copy(gone, gone, send_sem.at[slot]).wait()
-    for ch in range(CHUNKS):
+    for ch in range(BLOCKS):
         exchange(ch).wait_send()
     for k in range(owners):
         @pl.when(flat != (k % pairs) * tiles + 2 * k)
@@ -394,9 +389,8 @@
 def fused(tiles, pairs, state, target, perturbation, legendre, damp):
     members, levels, lats, lons = state.shape
     rows = levels * lats
-    part = rows // CHUNKS
-    width = levels // CHUNKS // 8 * 128
-    blocks = width // 128 * 2
+    part = rows // BLOCKS
+    width = 256
     flatten = lambda x: x.reshape(rows, lons)
     dma = pltpu.SemaphoreType.DMA
     grads, total = pl.pallas_call(
@@ -415,27 +409,27 @@
             pltpu.VMEM((2, 256, 2048), BF16),
             pltpu.VMEM((2, 256, 2048), BF16),
             pltpu.VMEM((2048, width), BF16),
-            pltpu.VMEM((CHUNKS, 256, width), F32),
-            pltpu.VMEM((CHUNKS, 2, 256, width), F32),
-            pltpu.VMEM((CHUNKS, 256, width), F32),
+            pltpu.VMEM((2, 256, width), F32),
+            pltpu.VMEM((2, 2, 256, width), F32),
+            pltpu.VMEM((2, 256, width), F32),
             pltpu.VMEM((rows, lons), F32),
-            pltpu.VMEM((CHUNKS, part, lons), BF16),
-            pltpu.VMEM((CHUNKS, part, lons), BF16),
+            pltpu.VMEM((BLOCKS, part, lons), BF16),
+            pltpu.VMEM((BLOCKS, part, lons), BF16),
             pltpu.VMEM((part, lons), BF16),
             pltpu.VMEM((part, lons), F32),
-            pltpu.VMEM((512, width), F32),
             pltpu.VMEM((512, 128), F32),
-            pltpu.VMEM((4 * CHUNKS, tiles, blocks, SIDE, 128), BF16),
-            pltpu.VMEM((4 * CHUNKS, tiles, blocks, SIDE, 128), BF16),
+            pltpu.VMEM((32 * STEP_IN, 128), F32),
+            pltpu.VMEM((4 * BLOCKS, tiles, 2, SIDE, 128), BF16),
+            pltpu.VMEM((4 * BLOCKS, tiles, 2, SIDE, 128), BF16),
             pltpu.VMEM((8, 8, 128), F32),
             pltpu.VMEM((tiles * pairs, 8, 128), F32),
             pltpu.VMEM((8, 128), F32),
             pltpu.VMEM((8, 8, 128), F32),
             dma((3,)),
-            dma((4 * CHUNKS,)),
-            dma((4 * CHUNKS,)),
-            dma((CHUNKS,)),
-            dma((CHUNKS,)),
+            dma((4 * BLOCKS,)),
+            dma((4 * BLOCKS,)),
+            dma((BLOCKS,)),
+            dma((BLOCKS,)),
             dma((9,)),
             dma((2,)),
         ],

time: 83.6 us -> 73.4 us (0.88)
  Pallas kernels: 74.4 us -> 64.2 us
    pallas_call x1, Pallas kernels: 74.4 us -> 64.2 us  [fused(): pl.pallas_call(functools.partial(kernel, tiles, pairs, levels), out_shape...]
where the time goes in v2:
time: 73.4 us; the launch traced here: 73 us
  Pallas kernels  64.2 us (87%)
  local copies, waits for them, and re-layouts  8.09 us (11%)
    pallas_call x1, Pallas kernels, fused(): pl.pallas_call(functools.partial(kernel, tiles, pairs, levels), out_shape...  64.2 us
    unnamed x14, local copies, waits for them, and re-layouts  8.09 us

profile of v2, /device:TPU:0, one launch (start us, length us, event | category | flops | bytes accessed | tf_op | source)
XLA Modules:
  0.0 73.0 jit_solution(11183677309681775757)
XLA Ops:
  0.6 0.0 copy-start
  0.6 1.6 %copy-done = bf16[16,256,256]{2,1,0:T(8,128)(2,1)S(1)} copy-done((bf16[16,256,256]{2,1,0:T(8,128)(2,1)S(1)}, bf16[16,256,256]{2,1,0:T(8,128)(2,1)}, u32[]{:S(2)}) %copy-start) | copy-done | bytes 2097176
  2.2 0.0 copy-start.1
  2.2 1.0 %copy-done.1 = bf16[1,32,16,512]{3,2,1,0:T(8,128)(2,1)S(1)} copy-done((bf16[1,32,16,512]{3,2,1,0:T(8,128)(2,1)S(1)}, bf16[1,32,16,512]{3,2,1,0:T(8,128)(2,1)}, u32[]{:S(2)}) %copy-start.1) | copy-done | bytes 524312
  3.3 0.0 copy-start.2
  3.3 1.0 %copy-done.2 = bf16[1,32,16,512]{3,2,1,0:T(8,128)(2,1)S(1)} copy-done((bf16[1,32,16,512]{3,2,1,0:T(8,128)(2,1)S(1)}, bf16[1,32,16,512]{3,2,1,0:T(8,128)(2,1)}, u32[]{:S(2)}) %copy-start.2) | copy-done | bytes 524312
  4.3 0.0 copy-start.3
  4.3 1.0 %copy-done.3 = bf16[1,32,16,512]{3,2,1,0:T(8,128)(2,1)S(1)} copy-done((bf16[1,32,16,512]{3,2,1,0:T(8,128)(2,1)S(1)}, bf16[1,32,16,512]{3,2,1,0:T(8,128)(2,1)}, u32[]{:S(2)}) %copy-start.3) | copy-done | bytes 524312
  5.3 0.0 copy-start.4
  5.4 1.0 %copy-done.4 = bf16[512,512]{1,0:T(8,128)(2,1)S(1)} copy-done((bf16[512,512]{1,0:T(8,128)(2,1)S(1)}, bf16[512,512]{1,0:T(8,128)(2,1)}, u32[]{:S(2)}) %copy-start.4) | copy-done | bytes 524312
  6.4 0.0 copy-start.5
  6.4 0.8 %copy-done.5 = f32[32,256]{1,0:T(8,128)S(1)} copy-done((f32[32,256]{1,0:T(8,128)S(1)}, f32[32,256]{1,0:T(8,128)}, u32[]{:S(2)}) %copy-start.5) | copy-done | bytes 32792
  7.2 64.2 %shard_map.77 = (f32[512,512]{1,0:T(8,128)S(1)}, f32[32,256]{1,0:T(8,128)S(1)}) custom-call(bf16[512,512]{1,0:T(8,128)(2,1)S(1)} %bitcast.5, bf16[512,512]{1,0:T(8,128)(2,1)S(1)} %copy-done.4, f32[32,256]{1,0:T(8,128)S(1)} %copy-done.5, bf16[512,512]{1,0:T(8,128)(2,1)S(1)} %bitcast.6, bf16[512,512]{1,0:T(8,128)(2,1)S(1)} %bitcast.7, ...), custom_call_target="tpu_custom_call" | custom-call | tf_op jit(solution)/shard_map/pallas_call | solution.py:396
  71.4 1.0 %copy.10 = f32[1,32,16,512]{3,2,1,0:T(8,128)} copy(f32[1,32,16,512]{3,2,1,0:T(8,128)S(1)} %bitcast.4) | data formatting | bytes 2097152
  72.4 0.6 copy.11
Async XLA Ops:
  0.6 1.6 %copy-start = (bf16[16,256,256]{2,1,0:T(8,128)(2,1)S(1)}, bf16[16,256,256]{2,1,0:T(8,128)(2,1)}, u32[]{:S(2)}) copy-start(bf16[16,256,256]{2,1,0:T(8,128)(2,1)} %leg_hbm.1) | copy-start | bytes 6291460
  2.2 1.0 %copy-start.1 = (bf16[1,32,16,512]{3,2,1,0:T(8,128)(2,1)S(1)}, bf16[1,32,16,512]{3,2,1,0:T(8,128)(2,1)}, u32[]{:S(2)}) copy-start(bf16[1,32,16,512]{3,2,1,0:T(8,128)(2,1)} %param.6) | copy-start | bytes 1572868
  3.3 1.0 %copy-start.2 = (bf16[1,32,16,512]{3,2,1,0:T(8,128)(2,1)S(1)}, bf16[1,32,16,512]{3,2,1,0:T(8,128)(2,1)}, u32[]{:S(2)}) copy-start(bf16[1,32,16,512]{3,2,1,0:T(8,128)(2,1)} %param.7) | copy-start | bytes 1572868
  4.3 1.0 %copy-start.3 = (bf16[1,32,16,512]{3,2,1,0:T(8,128)(2,1)S(1)}, bf16[1,32,16,512]{3,2,1,0:T(8,128)(2,1)}, u32[]{:S(2)}) copy-start(bf16[1,32,16,512]{3,2,1,0:T(8,128)(2,1)} %param.8) | copy-start | bytes 1572868
  5.3 1.0 %copy-start.4 = (bf16[512,512]{1,0:T(8,128)(2,1)S(1)}, bf16[512,512]{1,0:T(8,128)(2,1)}, u32[]{:S(2)}) copy-start(bf16[512,512]{1,0:T(8,128)(2,1)} %constant.2.clone.table) | copy-start | bytes 1572868
  6.4 0.8 %copy-start.5 = (f32[32,256]{1,0:T(8,128)S(1)}, f32[32,256]{1,0:T(8,128)}, u32[]{:S(2)}) copy-start(f32[32,256]{1,0:T(8,128)} %damp.1) | copy-start | bytes 98308

commit v3 on v2

--- a/solution.py
+++ b/solution.py
@@ -115,9 +115,9 @@
 
 def kernel(
     tiles, pairs, levels,
-    state, table, damp, target_hbm, pert_hbm, leg_hbm,
+    state_hbm, table_hbm, damp_hbm, target_hbm, pert_hbm, leg_hbm,
     out, total,
-    target, pert, leg, mk_n, mk_g, rhs, gain, coefs, dacc, bents, adv, other, gw, wave,
+    state, table, damp, target, pert, leg, mk_n, mk_g, rhs, gain, coefs, dacc, bents, adv, other, gw, wave,
     four, turned, send, recv, rs_src, rs_recv, ag_src, ag_recv,
     load_sem, send_sem, recv_sem, psend_sem, precv_sem, rs_sem, ag_sem,
 ):
@@ -129,12 +129,16 @@
     width = 256
     buddy = mine + 1 - 2 * lax.rem(mine, 2)
 
+    pairs_of_refs = (
+        (table_hbm, table), (state_hbm, state), (leg_hbm, leg),
+        (damp_hbm, damp), (pert_hbm, pert), (target_hbm, target),
+    )
     loads = [
         pltpu.make_async_copy(src, dst, load_sem.at[i])
-        for i, (src, dst) in enumerate(((leg_hbm, leg), (pert_hbm, pert), (target_hbm, target)))
+        for i, (src, dst) in enumerate(pairs_of_refs)
     ]
-    for load in loads:
-        load.start()
+    loads[0].start()
+    loads[1].start()
 
     barrier = pltpu.get_barrier_semaphore()
 
@@ -227,32 +231,88 @@
             device_id={"pair": buddy}, device_id_type=MESH,
         )
 
+    for load in loads[2:]:
+        load.start()
+
+    loads[0].wait()
+    loads[1].wait()
     for ch in range(BLOCKS):
         analyse(ch, state[pl.ds(ch * rows, rows), :])
         if ch == 0:
             pl.semaphore_wait(barrier, count - 1)
         all_to_all(ch)
 
-    loads[0].wait()
+    loads[2].wait()
     for i in range(16):
         degree = lax.broadcasted_iota(jnp.int32, (256, 256), 0)
         own = jnp.where(degree >= me * SIDE + i, leg[i].astype(F32), 0.0)
         at = pl.ds((i % 8) * 256, 256)
         mk_n[i // 8, :, at] = own.astype(BF16)
         mk_g[i // 8, :, at] = own.T.astype(BF16)
+    loads[3].wait()
     for ch in range(halves):
         gain[ch] = lax.dot_general(
             damp[...], pick(ch), (((0,), (0,)), ((), ())),
             precision=lax.Precision.HIGHEST, preferred_element_type=F32,
         )
-    loads[1].wait()
-    loads[2].wait()
+    loads[4].wait()
+    loads[5].wait()
+
+    owners = levels // 8 * 2
+    block = me // 2
+    owns = jnp.logical_and(lax.rem(me, 2) == 0, lax.rem(block, pairs) == mine)
+
+    def rs_copy(k):
+        return pltpu.make_async_remote_copy(
+            src_ref=rs_src.at[k], dst_ref=rs_recv.at[flat],
+            send_sem=rs_sem.at[1 + k], recv_sem=rs_sem.at[0],
+            device_id={"tile": 2 * k, "pair": k % pairs}, device_id_type=MESH,
+        )
+
+    def to_owners(half):
+        partial = lax.dot_general(
+            pick(half)[half * 16 : half * 16 + 16], dacc[half], (((1,), (1,)), ((), ())),
+            precision=lax.Precision.HIGHEST, preferred_element_type=F32,
+        )
+        for k in range(half * 4, half * 4 + 4):
+            row, col = k % 4 // 2 * 8, k % 2 * 128
+            rs_src[k] = partial[row : row + 8, col : col + 128]
+            is_owner = flat == (k % pairs) * tiles + 2 * k
+
+            @pl.when(jnp.logical_not(is_owner))
+            def _():
+                rs_copy(k).start()
+
+            @pl.when(is_owner)
+            def _():
+                pltpu.make_async_copy(rs_src.at[k], rs_recv.at[flat], rs_sem.at[0]).start()
+
+    def from_owners(half):
+        @pl.when(jnp.logical_and(owns, block // 4 == half))
+        def _():
+            pltpu.make_async_copy(rs_recv, rs_recv, rs_sem.at[0]).wait()
+            ag_src[...] = jnp.sum(rs_recv[...], axis=0)
+
+            def one(step, _):
+                to = lax.rem(flat + step, count)
+                pltpu.make_async_remote_copy(
+                    src_ref=ag_src, dst_ref=ag_recv.at[block],
+                    send_sem=ag_sem.at[1], recv_sem=ag_sem.at[0],
+                    device_id={"tile": lax.rem(to, tiles), "pair": to // tiles},
+                    device_id_type=MESH,
+                ).start()
+                return 0
+
+            lax.fori_loop(1, count, one, 0)
+            pltpu.make_async_copy(ag_src, ag_recv.at[block], ag_sem.at[0]).start()
 
     def through(phase, backward):
         for half in range(halves):
             for b in range(2):
                 arrived(phase * BLOCKS + 2 * half + b)
             spectral(half, phase, backward)
+            if backward:
+                to_owners(half)
             for b in range(2):
                 all_to_all((phase + 1) * BLOCKS + 2 * half + b)
 
@@ -304,64 +364,17 @@
 
     through(2, True)
 
-    partial = sum(
-        lax.dot_general(
-            pick(ch), dacc[ch], (((1,), (1,)), ((), ())),
-            precision=lax.Precision.HIGHEST, preferred_element_type=F32,
-        )
-        for ch in range(halves)
-    )
-    owners = levels // 8 * 2
-    for k in range(owners):
-        rs_src[k] = partial[k // 2 * 8 : k // 2 * 8 + 8, k % 2 * 128 : k % 2 * 128 + 128]
-
-    def rs_copy(k):
-        return pltpu.make_async_remote_copy(
-            src_ref=rs_src.at[k], dst_ref=rs_recv.at[flat],
-            send_sem=rs_sem.at[1 + k], recv_sem=rs_sem.at[0],
-            device_id={"tile": 2 * k, "pair": k % pairs}, device_id_type=MESH,
-        )
-
-    for k in range(owners):
-        is_owner = flat == (k % pairs) * tiles + 2 * k
-
-        @pl.when(jnp.logical_not(is_owner))
-        def _():
-            rs_copy(k).start()
-
-        @pl.when(is_owner)
-        def _():
-            pltpu.make_async_copy(rs_src.at[k], rs_recv.at[flat], rs_sem.at[0]).start()
-
-    block = me // 2
-    owns = jnp.logical_and(lax.rem(me, 2) == 0, lax.rem(block, pairs) == mine)
-
     def finish(ch):
         arrived(3 * BLOCKS + ch)
         synthesise(3 * BLOCKS + ch)
         at = pl.ds(ch * rows, rows)
         out[at, :] = out[at, :] + wave[...]
 
+    from_owners(0)
     finish(0)
-
-    @pl.when(owns)
-    def _():
-        pltpu.make_async_copy(rs_recv, rs_recv, rs_sem.at[0]).wait()
-        ag_src[...] = jnp.sum(rs_recv[...], axis=0)
-
-        def one(step, _):
-            to = lax.rem(flat + step, count)
-            pltpu.make_async_remote_copy(
-                src_ref=ag_src, dst_ref=ag_recv.at[block],
-                send_sem=ag_sem.at[1], recv_sem=ag_sem.at[0],
-                device_id={"tile": lax.rem(to, tiles), "pair": to // tiles}, device_id_type=MESH,
-            ).start()
-            return 0
-
-        lax.fori_loop(1, count, one, 0)
-        pltpu.make_async_copy(ag_src, ag_recv.at[block], ag_sem.at[0]).start()
-
-    for ch in range(1, BLOCKS):
+    finish(1)
+    from_owners(1)
+    for ch in range(2, BLOCKS):
         finish(ch)
 
     pltpu.make_async_copy(ag_recv, ag_recv, ag_sem.at[0]).wait()
@@ -399,10 +412,12 @@
             jax.ShapeDtypeStruct((rows, lons), F32),
             jax.ShapeDtypeStruct(damp.shape, F32),
         ),
-        in_specs=[pl.BlockSpec(memory_space=pltpu.VMEM)] * 3
-        + [pl.BlockSpec(memory_space=pl.ANY)] * 3,
+        in_specs=[pl.BlockSpec(memory_space=pltpu.HBM)] * 6,
         out_specs=(pl.BlockSpec(memory_space=pltpu.VMEM),) * 2,
         scratch_shapes=[
+            pltpu.VMEM((rows, lons), BF16),
+            pltpu.VMEM((2 * M, NLON), BF16),
+            pltpu.VMEM(damp.shape, F32),
             pltpu.VMEM((rows, lons), BF16),
             pltpu.VMEM((rows, lons), BF16),
             pltpu.VMEM(legendre.shape, BF16),
@@ -425,7 +440,7 @@
             pltpu.VMEM((tiles * pairs, 8, 128), F32),
             pltpu.VMEM((8, 128), F32),
             pltpu.VMEM((8, 8, 128), F32),
-            dma((3,)),
+            dma((6,)),
             dma((4 * BLOCKS,)),
             dma((4 * BLOCKS,)),
             dma((BLOCKS,)),

time: 73.4 us -> 70.3 us (0.958)
  Pallas kernels: 64.2 us -> 61.1 us
    pallas_call x1, Pallas kernels: 64.2 us -> 61.1 us  [fused(): pl.pallas_call(functools.partial(kernel, tiles, pairs, levels), out_shape...]
where the time goes in v3:
time: 70.3 us; the launch traced here: 69.9 us
  Pallas kernels  61.1 us (87%)
  local copies, waits for them, and re-layouts  8.09 us (12%)
    pallas_call x1, Pallas kernels, fused(): pl.pallas_call(functools.partial(kernel, tiles, pairs, levels), out_shape...  61.1 us
    unnamed x14, local copies, waits for them, and re-layouts  8.09 us

profile of v3, /device:TPU:0, one launch (start us, length us, event | category | flops | bytes accessed | tf_op | source)
XLA Modules:
  0.0 69.9 jit_solution(5643043566996607017)
XLA Ops:
  0.6 0.0 copy-start
  0.6 1.6 %copy-done = bf16[16,256,256]{2,1,0:T(8,128)(2,1)S(1)} copy-done((bf16[16,256,256]{2,1,0:T(8,128)(2,1)S(1)}, bf16[16,256,256]{2,1,0:T(8,128)(2,1)}, u32[]{:S(2)}) %copy-start) | copy-done | bytes 2097176
  2.2 0.0 copy-start.1
  2.2 1.0 %copy-done.1 = bf16[1,32,16,512]{3,2,1,0:T(8,128)(2,1)S(1)} copy-done((bf16[1,32,16,512]{3,2,1,0:T(8,128)(2,1)S(1)}, bf16[1,32,16,512]{3,2,1,0:T(8,128)(2,1)}, u32[]{:S(2)}) %copy-start.1) | copy-done | bytes 524312
  3.3 0.0 copy-start.2
  3.3 1.0 %copy-done.2 = bf16[1,32,16,512]{3,2,1,0:T(8,128)(2,1)S(1)} copy-done((bf16[1,32,16,512]{3,2,1,0:T(8,128)(2,1)S(1)}, bf16[1,32,16,512]{3,2,1,0:T(8,128)(2,1)}, u32[]{:S(2)}) %copy-start.2) | copy-done | bytes 524312
  4.3 0.0 copy-start.3
  4.3 1.0 %copy-done.3 = bf16[1,32,16,512]{3,2,1,0:T(8,128)(2,1)S(1)} copy-done((bf16[1,32,16,512]{3,2,1,0:T(8,128)(2,1)S(1)}, bf16[1,32,16,512]{3,2,1,0:T(8,128)(2,1)}, u32[]{:S(2)}) %copy-start.3) | copy-done | bytes 524312
  5.3 0.0 copy-start.4
  5.4 1.0 %copy-done.4 = bf16[512,512]{1,0:T(8,128)(2,1)S(1)} copy-done((bf16[512,512]{1,0:T(8,128)(2,1)S(1)}, bf16[512,512]{1,0:T(8,128)(2,1)}, u32[]{:S(2)}) %copy-start.4) | copy-done | bytes 524312
  6.4 0.0 copy-start.5
  6.4 0.8 %copy-done.5 = f32[32,256]{1,0:T(8,128)S(1)} copy-done((f32[32,256]{1,0:T(8,128)S(1)}, f32[32,256]{1,0:T(8,128)}, u32[]{:S(2)}) %copy-start.5) | copy-done | bytes 32792
  7.2 61.1 %shard_map.77 = (f32[512,512]{1,0:T(8,128)S(1)}, f32[32,256]{1,0:T(8,128)S(1)}) custom-call(bf16[512,512]{1,0:T(8,128)(2,1)S(1)} %bitcast.5, bf16[512,512]{1,0:T(8,128)(2,1)S(1)} %copy-done.4, f32[32,256]{1,0:T(8,128)S(1)} %copy-done.5, bf16[512,512]{1,0:T(8,128)(2,1)S(1)} %bitcast.6, bf16[512,512]{1,0:T(8,128)(2,1)S(1)} %bitcast.7, ...), custom_call_target="tpu_custom_call" | custom-call | tf_op jit(solution)/shard_map/pallas_call | solution.py:409
  68.3 1.0 %copy.10 = f32[1,32,16,512]{3,2,1,0:T(8,128)} copy(f32[1,32,16,512]{3,2,1,0:T(8,128)S(1)} %bitcast.4) | data formatting | bytes 2097152
  69.2 0.6 copy.11
Async XLA Ops:
  0.6 1.6 %copy-start = (bf16[16,256,256]{2,1,0:T(8,128)(2,1)S(1)}, bf16[16,256,256]{2,1,0:T(8,128)(2,1)}, u32[]{:S(2)}) copy-start(bf16[16,256,256]{2,1,0:T(8,128)(2,1)} %leg_hbm.1) | copy-start | bytes 6291460
  2.2 1.0 %copy-start.1 = (bf16[1,32,16,512]{3,2,1,0:T(8,128)(2,1)S(1)}, bf16[1,32,16,512]{3,2,1,0:T(8,128)(2,1)}, u32[]{:S(2)}) copy-start(bf16[1,32,16,512]{3,2,1,0:T(8,128)(2,1)} %param.6) | copy-start | bytes 1572868
  3.3 1.0 %copy-start.2 = (bf16[1,32,16,512]{3,2,1,0:T(8,128)(2,1)S(1)}, bf16[1,32,16,512]{3,2,1,0:T(8,128)(2,1)}, u32[]{:S(2)}) copy-start(bf16[1,32,16,512]{3,2,1,0:T(8,128)(2,1)} %param.7) | copy-start | bytes 1572868
  4.3 1.0 %copy-start.3 = (bf16[1,32,16,512]{3,2,1,0:T(8,128)(2,1)S(1)}, bf16[1,32,16,512]{3,2,1,0:T(8,128)(2,1)}, u32[]{:S(2)}) copy-start(bf16[1,32,16,512]{3,2,1,0:T(8,128)(2,1)} %param.8) | copy-start | bytes 1572868
  5.3 1.0 %copy-start.4 = (bf16[512,512]{1,0:T(8,128)(2,1)S(1)}, bf16[512,512]{1,0:T(8,128)(2,1)}, u32[]{:S(2)}) copy-start(bf16[512,512]{1,0:T(8,128)(2,1)} %constant.2.clone.table_hbm) | copy-start | bytes 1572868
  6.4 0.8 %copy-start.5 = (f32[32,256]{1,0:T(8,128)S(1)}, f32[32,256]{1,0:T(8,128)}, u32[]{:S(2)}) copy-start(f32[32,256]{1,0:T(8,128)} %damp_hbm.1) | copy-start | bytes 98308

commit v4 on v3

--- a/solution.py
+++ b/solution.py
@@ -116,10 +116,10 @@
 def kernel(
     tiles, pairs, levels,
     state_hbm, table_hbm, damp_hbm, target_hbm, pert_hbm, leg_hbm,
-    out, total,
-    state, table, damp, target, pert, leg, mk_n, mk_g, rhs, gain, coefs, dacc, bents, adv, other, gw, wave,
+    out_hbm, total,
+    out, state, table, damp, target, pert, leg, mk_n, mk_g, rhs, gain, coefs, dacc, bents, adv, other, gw, wave,
     four, turned, send, recv, rs_src, rs_recv, ag_src, ag_recv,
-    load_sem, send_sem, recv_sem, psend_sem, precv_sem, rs_sem, ag_sem,
+    load_sem, store_sem, send_sem, recv_sem, psend_sem, precv_sem, rs_sem, ag_sem,
 ):
     me, mine = lax.axis_index("tile"), lax.axis_index("pair")
     flat = mine * tiles + me
@@ -364,11 +364,16 @@
 
     through(2, True)
 
+    def store(ch):
+        at = pl.ds(ch * rows, rows)
+        return pltpu.make_async_copy(out.at[at, :], out_hbm.at[at, :], store_sem.at[ch])
+
     def finish(ch):
         arrived(3 * BLOCKS + ch)
         synthesise(3 * BLOCKS + ch)
         at = pl.ds(ch * rows, rows)
         out[at, :] = out[at, :] + wave[...]
+        store(ch).start()
 
     from_owners(0)
     finish(0)
@@ -382,6 +387,9 @@
         total[k // 2 * 8 : k // 2 * 8 + 8, k % 2 * 128 : k % 2 * 128 + 128] = ag_recv[k] * (
             (pairs * tiles * SIDE) ** (-0.5)
         )
+
+    for ch in range(BLOCKS):
+        store(ch).wait()
 
     for slot in range(4 * BLOCKS):
         gone = send.at[slot, pl.ds(0, tiles - 1)]
@@ -413,8 +421,12 @@
             jax.ShapeDtypeStruct(damp.shape, F32),
         ),
         in_specs=[pl.BlockSpec(memory_space=pltpu.HBM)] * 6,
-        out_specs=(pl.BlockSpec(memory_space=pltpu.VMEM),) * 2,
+        out_specs=(
+            pl.BlockSpec(memory_space=pl.ANY),
+            pl.BlockSpec(memory_space=pltpu.VMEM),
+        ),
         scratch_shapes=[
+            pltpu.VMEM((rows, lons), F32),
             pltpu.VMEM((rows, lons), BF16),
             pltpu.VMEM((2 * M, NLON), BF16),
             pltpu.VMEM(damp.shape, F32),
@@ -441,6 +453,7 @@
             pltpu.VMEM((8, 128), F32),
             pltpu.VMEM((8, 8, 128), F32),
             dma((6,)),
+            dma((BLOCKS,)),
             dma((4 * BLOCKS,)),
             dma((4 * BLOCKS,)),
             dma((BLOCKS,)),
@@ -449,7 +462,7 @@
             dma((2,)),
         ],
         compiler_params=pltpu.CompilerParams(
-            collective_id=0, has_side_effects=True, vmem_limit_bytes=48 * 2**20
+            collective_id=0, has_side_effects=True, vmem_limit_bytes=62 * 2**20
         ),
     )(
         flatten(state), jnp.asarray(table_rows(NLON, M)), damp,

time: 70.3 us -> 65.3 us (0.929)
  local copies, waits for them, and re-layouts: 8.09 us -> 2.93 us
    unnamed x14 -> x4, local copies, waits for them, and re-layouts: 8.09 us -> 2.93 us
where the time goes in v4:
time: 65.3 us; the launch traced here: 65.1 us
  Pallas kernels  61.5 us (94%)
  local copies, waits for them, and re-layouts  2.93 us (4%)
    pallas_call x1, Pallas kernels, fused(): pl.pallas_call(functools.partial(kernel, tiles, pairs, levels), out_shape...  61.5 us
    unnamed x4, local copies, waits for them, and re-layouts  2.93 us

profile of v4, /device:TPU:0, one launch (start us, length us, event | category | flops | bytes accessed | tf_op | source)
XLA Modules:
  0.0 65.1 jit_solution(9025263465594163325)
XLA Ops:
  0.6 61.5 %shard_map.77 = (f32[512,512]{1,0:T(8,128)}, f32[32,256]{1,0:T(8,128)}) custom-call(bf16[512,512]{1,0:T(8,128)(2,1)} %bitcast.5, bf16[512,512]{1,0:T(8,128)(2,1)} %constant.2.clone.table_hbm, f32[32,256]{1,0:T(8,128)} %damp_hbm.1, bf16[512,512]{1,0:T(8,128)(2,1)} %bitcast.6, bf16[512,512]{1,0:T(8,128)(2,1)} %bitcast.7, bf16[16,256,256]{2,1,0:T(8,128)(2,1)} %leg_hbm.1), custom_call_target="tpu_custom_call" | custom-call | tf_op jit(solution)/shard_map/pallas_call | solution.py:417
  62.2 0.0 copy-start
  62.2 2.3 %copy.10 = f32[1,32,16,512]{3,2,1,0:T(8,128)} copy(f32[1,32,16,512]{3,2,1,0:T(8,128)} %bitcast.4) | data formatting | bytes 2097152
  64.5 0.0 copy-done
  64.5 0.6 copy.11
Async XLA Ops:
  62.2 2.3 %copy-start = (f32[32,256]{1,0:T(8,128)S(1)}, f32[32,256]{1,0:T(8,128)}, u32[]{:S(2)}) copy-start(f32[32,256]{1,0:T(8,128)} %get-tuple-element.9) | copy-start | bytes 98308
